TPU v7x, 32 devices: a whole 2x2x4 slice. The times are simulated.
32 devices in a mesh: ctx: 16 (over z, y, core), head: 2 (over x).
Axes of the slice: x: 2, y: 2, z: 4, core: 2. Of those that a mesh axis runs over, the one named last changes fastest.
Arguments:
- queries: bfloat16 [64, 4096, 128], P(None, ('ctx', 'head')), may hold values from -6 to 6
- keys: bfloat16 [8, 4096, 128], P(None, ('ctx', 'head')), may hold values from -6 to 6
- values: bfloat16 [8, 4096, 128], P(None, ('ctx', 'head')), may hold values from -6 to 6
- delta: bfloat16 [64, 4096], P(None, ('ctx', 'head')), may hold values from -270 to 270
- grad_out: bfloat16 [64, 4096, 128], P(None, ('ctx', 'head')), may hold values from -24 to 24
- lse: bfloat16 [64, 4096], P(None, ('ctx', 'head')), may hold values from 6 to 8
Outputs:
- query_grads: bfloat16 [64, 4096, 128], P(None, ('ctx', 'head'))
- key_grads: bfloat16 [8, 4096, 128], P(None, ('ctx', 'head'))
- value_grads: bfloat16 [8, 4096, 128], P(None, ('ctx', 'head'))
All inputs are finite; a program needn't handle non-finite values.
Results may differ from a plain program's by a relative error of at most 0.005.
Values may be sent and summed in bfloat16 or wider, within the bound.
A program may use at most 128 MiB of HBM per device.

v0:
```python
import math

import jax
import jax.numpy as jnp
from jax import lax
from jax.sharding import PartitionSpec as P


def from_behind(block, axis, distance):
    devices = range(lax.axis_size(axis))
    route = [(i - distance, i) for i in devices if i - distance in devices]
    return lax.ppermute(block, axis, route)


def tile_grads(queries, delta, grads_out, lse, keys, values, allowed):
    heads, rows, width = queries.shape
    groups = keys.shape[0]
    ratio = heads // groups
    scale = 1.0 / math.sqrt(width)
    q_four = queries.reshape(groups, ratio, rows, width)
    g_four = grads_out.reshape(groups, ratio, rows, width)
    delta_f = delta.astype(jnp.float32).reshape(groups, ratio, rows)
    scores = jnp.einsum("kgrd,kjd->kgrj", q_four, keys, preferred_element_type=jnp.float32) * scale
    probs = jnp.exp(scores - lse.astype(jnp.float32).reshape(groups, ratio, rows)[..., None])
    if allowed is not None:
        probs = jnp.where(allowed, probs, 0.0)
    probs_half = probs.astype(jnp.bfloat16)
    dvalue = jnp.einsum("kgrj,kgrd->kjd", probs_half, g_four, preferred_element_type=jnp.float32)
    dprobs = jnp.einsum("kgrd,kjd->kgrj", g_four, values, preferred_element_type=jnp.float32)
    dscores = (probs * (dprobs - delta_f[..., None])).astype(jnp.bfloat16)
    dquery = jnp.einsum("kgrj,kjd->kgrd", dscores, keys, preferred_element_type=jnp.float32) * scale
    dkey = jnp.einsum("kgrj,kgrd->kjd", dscores, q_four, preferred_element_type=jnp.float32) * scale
    return (dquery.reshape(heads, rows, width), dkey, dvalue)


def local(queries, keys, values, delta, grad_out, lse):
    cycle_size = lax.axis_size("ctx")
    offset = cycle_size // 2
    is_late = lax.axis_index("ctx") >= offset
    q_loc, d_loc, g_loc, l_loc, k_loc, v_loc = (
        lax.all_to_all(queries, "head", split_axis=0, concat_axis=1, tiled=True),
        lax.all_to_all(delta, "head", split_axis=0, concat_axis=1, tiled=True),
        lax.all_to_all(grad_out, "head", split_axis=0, concat_axis=1, tiled=True),
        lax.all_to_all(lse, "head", split_axis=0, concat_axis=1, tiled=True),
        lax.all_to_all(keys, "head", split_axis=0, concat_axis=1, tiled=True),
        lax.all_to_all(values, "head", split_axis=0, concat_axis=1, tiled=True),
    )
    rows = q_loc.shape[1]
    query_pos = jnp.arange(rows, dtype=jnp.int32)
    key_pos = jnp.arange(k_loc.shape[1], dtype=jnp.int32)
    allowed = key_pos[None, :] <= query_pos[:, None]
    dq_near, dk_near, dv_near = tile_grads(q_loc, d_loc, g_loc, l_loc, k_loc, v_loc, allowed)
    k_far, v_far = from_behind((k_loc, v_loc), "ctx", offset)
    half = rows // 2
    sent = from_behind(
        (q_loc[:, half:], d_loc[:, half:], g_loc[:, half:], l_loc[:, half:]), "ctx", -offset
    )

    def late_work():
        return tile_grads(
            q_loc[:, :half], d_loc[:, :half], g_loc[:, :half], l_loc[:, :half], k_far, v_far, None
        )

    def early_work():
        return tile_grads(sent[0], sent[1], sent[2], sent[3], k_loc, v_loc, None)

    dq_part, dk_send, dv_send = lax.cond(is_late, late_work, early_work)
    dq_recv = from_behind(dq_part, "ctx", offset)
    dq_far = jnp.where(is_late, jnp.concatenate([dq_part, dq_recv], 1), 0.0)
    dk_keep = jnp.where(is_late, 0.0, dk_send)
    dv_keep = jnp.where(is_late, 0.0, dv_send)
    dk_recv, dv_recv = from_behind((dk_send, dv_send), "ctx", -offset)
    query_grads = (dq_near + dq_far).astype(jnp.bfloat16)
    dk_total = dk_near + (dk_keep + dk_recv)
    dv_total = dv_near + (dv_keep + dv_recv)
    return (
        lax.all_to_all(query_grads, "head", split_axis=1, concat_axis=0, tiled=True),
        lax.all_to_all(
            dk_total.astype(jnp.bfloat16), "head", split_axis=1, concat_axis=0, tiled=True
        ),
        lax.all_to_all(
            dv_total.astype(jnp.bfloat16), "head", split_axis=1, concat_axis=0, tiled=True
        ),
    )


def solution(mesh):
    return jax.shard_map(
        local,
        mesh=mesh,
        in_specs=(
            P(None, ("ctx", "head"), None),
            P(None, ("ctx", "head"), None),
            P(None, ("ctx", "head"), None),
            P(None, ("ctx", "head")),
            P(None, ("ctx", "head"), None),
            P(None, ("ctx", "head")),
        ),
        out_specs=(
            P(None, ("ctx", "head"), None),
            P(None, ("ctx", "head"), None),
            P(None, ("ctx", "head"), None),
        ),
        check_vma=False,
    )
```

profile of v0, /device:TPU:0, one launch (start us, length us, event | category | flops | bytes accessed | tf_op | source)
XLA Modules:
  0.0 287.7 jit_solution(14389311338088861386)
XLA Ops:
  0.6 8.1 %all_to_all.164 = bf16[2,32,128]{2,1,0:T(8,128)(2,1)S(1)} all-to-all(bf16[2,32,128]{2,1,0:T(8,128)(2,1)} %bitcast.174), channel_id=1, replica_groups=mesh['ctx'=16,'head'=2] {'head'}, dimensions={0} | all-to-all | bytes 32768 | tf_op jit(solution)/shard_map/all_to_all | solution.py:44
  8.7 7.1 %all_to_all.165 = bf16[2,32,128]{2,1,0:T(8,128)(2,1)S(1)} all-to-all(bf16[2,32,128]{2,1,0:T(8,128)(2,1)} %bitcast.175), channel_id=1, replica_groups=mesh['ctx'=16,'head'=2] {'head'}, dimensions={0} | all-to-all | bytes 32768 | tf_op jit(solution)/shard_map/all_to_all | solution.py:42
  15.8 8.6 %all_to_all.166 = bf16[8,128,128]{2,1,0:T(8,128)(2,1)S(1)} all-to-all(bf16[8,128,128]{2,1,0:T(8,128)(2,1)} %param.9), channel_id=1, replica_groups=mesh['ctx'=16,'head'=2] {'head'}, dimensions={0} | all-to-all | bytes 524288 | tf_op jit(solution)/shard_map/all_to_all | solution.py:45
  24.4 8.6 %all_to_all.167 = bf16[8,128,128]{2,1,0:T(8,128)(2,1)S(1)} all-to-all(bf16[8,128,128]{2,1,0:T(8,128)(2,1)} %param.10), channel_id=1, replica_groups=mesh['ctx'=16,'head'=2] {'head'}, dimensions={0} | all-to-all | bytes 524288 | tf_op jit(solution)/shard_map/all_to_all | solution.py:46
  33.0 26.4 %all_to_all.168 = bf16[64,128,128]{2,1,0:T(8,128)(2,1)} all-to-all(bf16[64,128,128]{2,1,0:T(8,128)(2,1)} %param.8), channel_id=1, replica_groups=mesh['ctx'=16,'head'=2] {'head'}, dimensions={0} | all-to-all | bytes 4194304 | tf_op jit(solution)/shard_map/all_to_all | solution.py:41
  59.4 4.8 %all-to-all-start.3 = ((bf16[64,128,128]{2,1,0:T(8,128)(2,1)}), bf16[64,128,128]{2,1,0:T(8,128)(2,1)}, u32[]{:S(2)}, u32[]{:S(2)}) async-start(bf16[64,128,128]{2,1,0:T(8,128)(2,1)} %param.12), calls=%async_computation.3 | async-start | bytes 4194304 | tf_op jit(solution)/shard_map/all_to_all | solution.py:43
  68.4 7.3 %collective-permute-start.4 = (bf16[4,256,128]{2,1,0:T(8,128)(2,1)S(1)}, bf16[4,256,128]{2,1,0:T(8,128)(2,1)}, u32[]{:S(2)}, u32[]{:S(2)}) collective-permute-start(bf16[4,256,128]{2,1,0:T(8,128)(2,1)S(1)} %bitcast.156), channel_id=1, source_target_pairs={{0,16},{2,18},{4,20},{6,22},{8,24},{10,26},{12,28},{14,30},{1,17},... | collective-permute-start | bytes 786440 | tf_op jit(solution)/shard_map/ppermute | solution.py:12
  75.7 1.8 copy.45
  79.9 4.2 %all-to-all-done.3 = bf16[64,128,128]{2,1,0:T(8,128)(2,1)} async-done(((bf16[64,128,128]{2,1,0:T(8,128)(2,1)}), bf16[64,128,128]{2,1,0:T(8,128)(2,1)}, u32[]{:S(2)}, u32[]{:S(2)}) %all-to-all-start.3) | async-done | bytes 2097184 | tf_op jit(solution)/shard_map/all_to_all | solution.py:43
  84.1 1.7 copy.48
  88.6 5.5 %collective-permute-start.5 = (bf16[4,256,128]{2,1,0:T(8,128)(2,1)S(1)}, bf16[4,256,128]{2,1,0:T(8,128)(2,1)S(1)}, u32[]{:S(2)}, u32[]{:S(2)}) collective-permute-start(bf16[4,256,128]{2,1,0:T(8,128)(2,1)S(1)} %bitcast.169), channel_id=1, source_target_pairs={{0,16},{2,18},{4,20},{6,22},{8,24},{10,26},{12,28},{14,30},{1,17},... | collective-permute-start | bytes 786440 | tf_op jit(solution)/shard_map/ppermute | solution.py:12
  94.1 4.5 %multiply_convert_fusion.2 = bf16[4,8,256,256]{3,2,1,0:T(8,128)(2,1)} fusion(f32[4,8,256,256]{3,2,1,0:T(8,128)S(1)} %fusion.38, f32[4,8,256]{2,1,0:T(8,128)S(1)} %copy-done.6, f32[4,8,256]{2,1,0:T(8,128)S(1)} %reshape.74, pred[256,256]{1,0:T(8,128)(4,1)S(1)} %iota_compare_fusion, bf16[4,8,256,128]{3,2,1,0:T(8,128)(2,1)S(1)} %bitcast.151, ...), kind=kOutput, calls=%fused_computation.30 | convolution fusion | flops 549453824 | bytes 15073280 | tf_op jit(solution)/shard_map/kgrd,kjd->kgrj/dot_general | solution.py:29
  98.6 70.7 %collective-permute-done = bf16[32,128,128]{2,1,0:T(8,128)(2,1)S(1)} collective-permute-done((bf16[32,128,128]{2,1,0:T(8,128)(2,1)}, bf16[32,128,128]{2,1,0:T(8,128)(2,1)S(1)}, u32[]{:S(2)}, u32[]{:S(2)}) %collective-permute-start) | collective-permute-done | bytes 1048608 | tf_op jit(solution)/shard_map/ppermute | solution.py:12
  169.3 21.3 %collective-permute-done.2 = bf16[32,128,128]{2,1,0:T(8,128)(2,1)S(1)} collective-permute-done((bf16[32,128,128]{2,1,0:T(8,128)(2,1)S(1)}, bf16[32,128,128]{2,1,0:T(8,128)(2,1)S(1)}, u32[]{:S(2)}, u32[]{:S(2)}) %collective-permute-start.2) | collective-permute-done | bytes 1048608 | tf_op jit(solution)/shard_map/ppermute | solution.py:12
  190.6 9.9 %conditional.1 = (f32[4,256,128]{2,1,0:T(8,128)S(1)}, f32[4,256,128]{2,1,0:T(8,128)S(1)}, f32[4,8,128,128]{3,2,1,0:T(8,128)}, f32[]{:T(128)}) conditional(s32[]{:T(128)} %convert_element_type.67, (bf16[32,128,128]{2,1,0:T(8,128)(2,1)S(1)}, bf16[4,256,128]{2,1,0:T(8,128)(2,1)S(1)}, bf16[32,128]{1,0:T(8,128)(2,1)}, bf16[32,128,128]{2,1,0:T(8,128)(2,1)S(1)}, ...), branch_computations={%region_0.1_spmd, %region_1.2_spmd} | conditional | flops 1350574080 | bytes 31293508 | solution.py:67
  193.7 2.0 fusion.9
  195.8 2.1 convolution_bitcast_fusion
  197.9 2.6 fusion.5
  200.5 1.9 broadcast_multiply_fusion
  202.4 2.5 copy.86
  204.9 3.2 %collective-permute-start.6 = (f32[32,128,128]{2,0,1:T(8,128)}, f32[32,128,128]{2,0,1:T(8,128)}, u32[]{:S(2)}, u32[]{:S(2)}) collective-permute-start(f32[32,128,128]{2,0,1:T(8,128)} %bitcast.140), channel_id=1, source_target_pairs={{0,16},{2,18},{4,20},{6,22},{8,24},{10,26},{12,28},{14,30},{1,17},... | collective-permute-start | bytes 6291464 | tf_op jit(solution)/shard_map/ppermute | solution.py:12
  208.2 5.2 %fusion.32 = f32[4,256,128]{2,1,0:T(8,128)} fusion(bf16[4,8,256,128]{3,2,1,0:T(8,128)(2,1)} %bitcast.153, f32[4,8,256,256]{3,2,1,0:T(8,128)S(1)} %copy-done.2, f32[4,8,256]{2,1,0:T(8,128)S(1)} %reshape.74, pred[256,256]{1,0:T(8,128)(4,1)S(1)} %iota_compare_fusion), kind=kOutput, calls=%fused_computation.40 | convolution fusion | flops 545259520 | bytes 11108352 | tf_op jit(solution)/shard_map/kgrj,kgrd->kjd/dot_general | solution.py:28
  214.7 3.2 %convolution_multiply_fusion = f32[4,8,256,128]{3,2,1,0:T(8,128)} fusion(bf16[4,8,256,256]{3,2,1,0:T(8,128)(2,1)S(1)} %copy-done, bf16[4,256,128,1]{2,1,3,0:T(8,128)(2,1)S(1)} %bitcast.159), kind=kOutput, calls=%fused_computation.38 | convolution fusion | flops 537919488 | bytes 8650752 | tf_op jit(solution)/shard_map/kgrj,kjd->kgrd/dot_general | solution.py:31
  220.8 10.2 %collective-permute-done.7 = f32[4,256,128]{2,1,0:T(8,128)S(1)} collective-permute-done((f32[4,256,128]{2,1,0:T(8,128)S(1)}, f32[4,256,128]{2,1,0:T(8,128)S(1)}, u32[]{:S(2)}, u32[]{:S(2)}) %collective-permute-start.7) | collective-permute-done | bytes 524320 | tf_op jit(solution)/shard_map/ppermute | solution.py:12
  232.1 3.4 %all-to-all-start.7 = ((bf16[4,256,128]{2,0,1:T(4,128)(2,1)}), bf16[4,256,128]{2,0,1:T(4,128)(2,1)S(1)}, u32[]{:S(2)}, u32[]{:S(2)}) async-start(bf16[4,256,128]{2,0,1:T(4,128)(2,1)} %copy.57), calls=%async_computation.7 | async-start | bytes 524288 | tf_op jit(solution)/shard_map/all_to_all | solution.py:78
  235.5 4.4 %collective-permute-done.8 = f32[4,256,128]{2,1,0:T(8,128)} collective-permute-done((f32[4,256,128]{2,1,0:T(8,128)S(1)}, f32[4,256,128]{2,1,0:T(8,128)}, u32[]{:S(2)}, u32[]{:S(2)}) %collective-permute-start.8) | collective-permute-done | bytes 524320 | tf_op jit(solution)/shard_map/ppermute | solution.py:12
  242.2 3.4 %all-to-all-start.8 = ((bf16[4,256,128]{2,0,1:T(4,128)(2,1)}), bf16[4,256,128]{2,0,1:T(4,128)(2,1)S(1)}, u32[]{:S(2)}, u32[]{:S(2)}) async-start(bf16[4,256,128]{2,0,1:T(4,128)(2,1)} %copy.60), calls=%async_computation.8 | async-start | bytes 524288 | tf_op jit(solution)/shard_map/all_to_all | solution.py:81
  245.6 5.5 %collective-permute-done.6 = f32[32,128,128]{2,0,1:T(8,128)} collective-permute-done((f32[32,128,128]{2,0,1:T(8,128)}, f32[32,128,128]{2,0,1:T(8,128)}, u32[]{:S(2)}, u32[]{:S(2)}) %collective-permute-start.6) | collective-permute-done | bytes 2097184 | tf_op jit(solution)/shard_map/ppermute | solution.py:12
  251.1 7.4 %fusion.28 = bf16[32,256,128]{2,0,1:T(8,128)(2,1)} fusion(f32[32,128,128]{2,0,1:T(8,128)} %collective-permute-done.6, f32[32,128,128]{2,0,1:T(8,128)} %bitcast.140, f32[32,256,128]{2,1,0:T(8,128)} %bitcast.145, pred[]{:T(512)S(6)} %ge.3), kind=kLoop, calls=%fused_computation.35 | loop fusion | flops 4194304 | bytes 10485761 | tf_op jit(solution)/shard_map/convert_element_type | solution.py:73
  258.5 3.8 %all-to-all-start.6 = ((bf16[32,256,128]{2,0,1:T(8,128)(2,1)}), bf16[32,256,128]{2,0,1:T(8,128)(2,1)S(1)}, u32[]{:S(2)}, u32[]{:S(2)}) async-start(bf16[32,256,128]{2,0,1:T(8,128)(2,1)} %fusion.28), calls=%async_computation.6 | async-start | bytes 4194304 | tf_op jit(solution)/shard_map/all_to_all | solution.py:77
  263.8 21.8 %all-to-all-done.6 = bf16[32,256,128]{2,0,1:T(8,128)(2,1)S(1)} async-done(((bf16[32,256,128]{2,0,1:T(8,128)(2,1)}), bf16[32,256,128]{2,0,1:T(8,128)(2,1)S(1)}, u32[]{:S(2)}, u32[]{:S(2)}) %all-to-all-start.6) | async-done | bytes 2097184 | tf_op jit(solution)/shard_map/all_to_all | solution.py:77
  285.6 2.1 copy.55
  (53 shorter events, 21.2 us)
Async XLA Ops:
  59.4 24.7 %all-to-all-start.3 = ((bf16[64,128,128]{2,1,0:T(8,128)(2,1)}), bf16[64,128,128]{2,1,0:T(8,128)(2,1)}, u32[]{:S(2)}, u32[]{:S(2)}) async-start(bf16[64,128,128]{2,1,0:T(8,128)(2,1)} %param.12), calls=%async_computation.3 | async-start | bytes 4194304 | tf_op jit(solution)/shard_map/all_to_all | solution.py:43
  64.3 34.3 %collective-permute-start.1 = (bf16[32,128]{1,0:T(8,128)(2,1)S(1)}, bf16[32,128]{1,0:T(8,128)(2,1)}, u32[]{:S(2)}, u32[]{:S(2)}) collective-permute-start(bf16[32,128]{1,0:T(8,128)(2,1)S(1)} %slice.33), channel_id=1, source_target_pairs={{16,0},{18,2},{20,4},{22,6},{24,8},{26,10},{28,12},{30,14},{17,1},... | collective-permute-start | bytes 24584 | tf_op jit(solution)/shard_map/ppermute | solution.py:12
  65.6 33.0 %collective-permute-start.3 = (bf16[32,128]{1,0:T(8,128)(2,1)S(1)}, bf16[32,128]{1,0:T(8,128)(2,1)}, u32[]{:S(2)}, u32[]{:S(2)}) collective-permute-start(bf16[32,128]{1,0:T(8,128)(2,1)S(1)} %slice.35), channel_id=1, source_target_pairs={{16,0},{18,2},{20,4},{22,6},{24,8},{26,10},{28,12},{30,14},{17,1},... | collective-permute-start | bytes 24584 | tf_op jit(solution)/shard_map/ppermute | solution.py:12
  68.4 20.1 %collective-permute-start.4 = (bf16[4,256,128]{2,1,0:T(8,128)(2,1)S(1)}, bf16[4,256,128]{2,1,0:T(8,128)(2,1)}, u32[]{:S(2)}, u32[]{:S(2)}) collective-permute-start(bf16[4,256,128]{2,1,0:T(8,128)(2,1)S(1)} %bitcast.156), channel_id=1, source_target_pairs={{0,16},{2,18},{4,20},{6,22},{8,24},{10,26},{12,28},{14,30},{1,17},... | collective-permute-start | bytes 786440 | tf_op jit(solution)/shard_map/ppermute | solution.py:12
  78.7 90.6 %collective-permute-start = (bf16[32,128,128]{2,1,0:T(8,128)(2,1)}, bf16[32,128,128]{2,1,0:T(8,128)(2,1)S(1)}, u32[]{:S(2)}, u32[]{:S(2)}) collective-permute-start(bf16[32,128,128]{2,1,0:T(8,128)(2,1)} %slice.32), channel_id=1, source_target_pairs={{16,0},{18,2},{20,4},{22,6},{24,8},{26,10},{28,12},{30,14},{17,1},... | collective-permute-start | bytes 3145736 | tf_op jit(solution)/shard_map/ppermute | solution.py:12
  85.8 104.7 %copy-start.3 = (bf16[2,32,128,128]{3,2,0,1:T(8,128)(2,1)}, bf16[2,32,128,128]{3,2,0,1:T(8,128)(2,1)S(1)}, u32[]{:S(2)}) copy-start(bf16[2,32,128,128]{3,2,0,1:T(8,128)(2,1)S(1)} %copy.48) | copy-start | bytes 6291460
  86.0 104.6 %collective-permute-start.2 = (bf16[32,128,128]{2,1,0:T(8,128)(2,1)S(1)}, bf16[32,128,128]{2,1,0:T(8,128)(2,1)S(1)}, u32[]{:S(2)}, u32[]{:S(2)}) collective-permute-start(bf16[32,128,128]{2,1,0:T(8,128)(2,1)S(1)} %slice.34), channel_id=1, source_target_pairs={{16,0},{18,2},{20,4},{22,6},{24,8},{26,10},{28,12},{30,14},{17,1},... | collective-permute-start | bytes 3145736 | tf_op jit(solution)/shard_map/ppermute | solution.py:12
  87.3 1.3 copy-start.5
  87.3 6.8 %copy-start.6 = (f32[4,8,256]{2,1,0:T(8,128)S(1)}, f32[4,8,256]{2,1,0:T(8,128)}, u32[]{:S(2)}) copy-start(f32[4,8,256]{2,1,0:T(8,128)} %reshape.75) | copy-start | bytes 98308
  88.5 10.1 %copy-start.1 = (f32[4,8,256,256]{3,2,1,0:T(8,128)}, f32[4,8,256,256]{3,2,1,0:T(8,128)S(1)}, u32[]{:S(2)}) copy-start(f32[4,8,256,256]{3,2,1,0:T(8,128)S(1)} %fusion.38) | copy-start | bytes 25165828
  88.6 10.1 %collective-permute-start.5 = (bf16[4,256,128]{2,1,0:T(8,128)(2,1)S(1)}, bf16[4,256,128]{2,1,0:T(8,128)(2,1)S(1)}, u32[]{:S(2)}, u32[]{:S(2)}) collective-permute-start(bf16[4,256,128]{2,1,0:T(8,128)(2,1)S(1)} %bitcast.169), channel_id=1, source_target_pairs={{0,16},{2,18},{4,20},{6,22},{8,24},{10,26},{12,28},{14,30},{1,17},... | collective-permute-start | bytes 786440 | tf_op jit(solution)/shard_map/ppermute | solution.py:12
  190.6 3.1 %copy-start.4 = (bf16[32,128,128]{2,1,0:T(8,128)(2,1)}, bf16[32,128,128]{2,1,0:T(8,128)(2,1)S(1)}, u32[]{:S(2)}) copy-start(bf16[32,128,128]{2,1,0:T(8,128)(2,1)S(1)} %get-tuple-element.49) | copy-start | bytes 3145732 | tf_op jit(solution)/shard_map/cond
  200.5 7.7 %copy-start.2 = (f32[4,8,256,256]{3,2,1,0:T(8,128)S(1)}, f32[4,8,256,256]{3,2,1,0:T(8,128)}, u32[]{:S(2)}) copy-start(f32[4,8,256,256]{3,2,1,0:T(8,128)} %copy-done.1) | copy-start | bytes 25165828
  204.9 9.8 %copy-start = (bf16[4,8,256,256]{3,2,1,0:T(8,128)(2,1)S(1)}, bf16[4,8,256,256]{3,2,1,0:T(8,128)(2,1)}, u32[]{:S(2)}) copy-start(bf16[4,8,256,256]{3,2,1,0:T(8,128)(2,1)} %multiply_convert_fusion.2) | copy-start | bytes 12582916
  204.9 46.2 %collective-permute-start.6 = (f32[32,128,128]{2,0,1:T(8,128)}, f32[32,128,128]{2,0,1:T(8,128)}, u32[]{:S(2)}, u32[]{:S(2)}) collective-permute-start(f32[32,128,128]{2,0,1:T(8,128)} %bitcast.140), channel_id=1, source_target_pairs={{0,16},{2,18},{4,20},{6,22},{8,24},{10,26},{12,28},{14,30},{1,17},... | collective-permute-start | bytes 6291464 | tf_op jit(solution)/shard_map/ppermute | solution.py:12
  213.4 17.7 %collective-permute-start.7 = (f32[4,256,128]{2,1,0:T(8,128)S(1)}, f32[4,256,128]{2,1,0:T(8,128)S(1)}, u32[]{:S(2)}, u32[]{:S(2)}) collective-permute-start(f32[4,256,128]{2,1,0:T(8,128)S(1)} %broadcast_multiply_fusion.1), channel_id=1, source_target_pairs={{16,0},{18,2},{20,4},{22,6},{24,8},{26,10},{28,12},{30,14},{17,1},... | collective-permute-start | bytes 1572872 | tf_op jit(solution)/shard_map/ppermute | solution.py:12
  217.9 22.0 %collective-permute-start.8 = (f32[4,256,128]{2,1,0:T(8,128)S(1)}, f32[4,256,128]{2,1,0:T(8,128)}, u32[]{:S(2)}, u32[]{:S(2)}) collective-permute-start(f32[4,256,128]{2,1,0:T(8,128)S(1)} %get-tuple-element.71), channel_id=1, source_target_pairs={{16,0},{18,2},{20,4},{22,6},{24,8},{26,10},{28,12},{30,14},{17,1},... | collective-permute-start | bytes 1572872 | tf_op jit(solution)/shard_map/ppermute | solution.py:12
  232.1 10.1 %all-to-all-start.7 = ((bf16[4,256,128]{2,0,1:T(4,128)(2,1)}), bf16[4,256,128]{2,0,1:T(4,128)(2,1)S(1)}, u32[]{:S(2)}, u32[]{:S(2)}) async-start(bf16[4,256,128]{2,0,1:T(4,128)(2,1)} %copy.57), calls=%async_computation.7 | async-start | bytes 524288 | tf_op jit(solution)/shard_map/all_to_all | solution.py:78
  242.2 16.4 %all-to-all-start.8 = ((bf16[4,256,128]{2,0,1:T(4,128)(2,1)}), bf16[4,256,128]{2,0,1:T(4,128)(2,1)S(1)}, u32[]{:S(2)}, u32[]{:S(2)}) async-start(bf16[4,256,128]{2,0,1:T(4,128)(2,1)} %copy.60), calls=%async_computation.8 | async-start | bytes 524288 | tf_op jit(solution)/shard_map/all_to_all | solution.py:81
  258.5 27.0 %all-to-all-start.6 = ((bf16[32,256,128]{2,0,1:T(8,128)(2,1)}), bf16[32,256,128]{2,0,1:T(8,128)(2,1)S(1)}, u32[]{:S(2)}, u32[]{:S(2)}) async-start(bf16[32,256,128]{2,0,1:T(8,128)(2,1)} %fusion.28), calls=%async_computation.6 | async-start | bytes 4194304 | tf_op jit(solution)/shard_map/all_to_all | solution.py:77
where the time goes:
time: 289 us; the launch traced here: 288 us
  waiting for transfers between devices  138 us (48%)
  blocking collectives  58.7 us (20%)
  starting transfers between devices  39.3 us (14%)
  matrix products  24.9 us (9%)
  local copies, waits for them, and re-layouts  14.2 us (5%)
  other arithmetic  11.5 us (4%)
    ppermute x9, waiting for transfers between devices, from_behind(): return lax.ppermute(block, axis, route)  112 us
    all_to_all x1, blocking collectives, local(): lax.all_to_all(queries, 'head', split_axis=0, concat_axis=1, tiled=True)  26.4 us
    ppermute x9, starting transfers between devices, from_behind(): return lax.ppermute(block, axis, route)  23.8 us
    all_to_all x1, waiting for transfers between devices, local(): lax.all_to_all(query_grads, 'head', split_axis=1, concat_axis=0, tiled=True)  21.8 us
    all_to_all x1, blocking collectives, local(): lax.all_to_all(keys, 'head', split_axis=0, concat_axis=1, tiled=True)  8.6 us
    all_to_all x1, blocking collectives, local(): lax.all_to_all(values, 'head', split_axis=0, concat_axis=1, tiled=True)  8.6 us
    all_to_all x1, blocking collectives, local(): lax.all_to_all(lse, 'head', split_axis=0, concat_axis=1, tiled=True)  8.07 us
    dot_general x2, matrix products, tile_grads(): jnp.einsum('kgrj,kgrd->kjd', probs_half, g_four, preferred_element_type=j...  7.81 us
  transfers between devices with their start and end apart: 13, of which 7 were waited for; matrix products, arithmetic and copies ran while one was open for 12% of the time, Pallas kernels for 0%

commit v1 on v0

v1 whole, which is shorter than its diff:
```python
import functools
import math

import jax
import jax.numpy as jnp
from jax import lax
from jax.experimental import pallas as pl
from jax.experimental.pallas import tpu as pltpu
from jax.sharding import PartitionSpec as P

F32 = jnp.float32
BF16 = jnp.bfloat16
MESH = pl.DeviceIdType.MESH
LOG2E = 1.0 / math.log(2.0)
NEAR, FAR, RELAY, NEAR_BACK, SWAP, FAR_BACK = range(6)


def dot(a, b, dims):
    return lax.dot_general(a, b, (dims, ((), ())), preferred_element_type=F32)


NT = ((1,), (1,))
NN = ((1,), (0,))


def kernel(
    n_ctx,
    q_hbm, k_ref, v_ref, delta_ref, g_hbm, lse_ref,
    dq_hbm, dk_ref, dv_ref,
    q_ref, g_ref, dq_ref, dq_acc, lse2, delta_f,
    own_kv, near_kv, far_kv, relay_kv,
    near_acc, far_acc,
    near_send, near_recv, swap_send, swap_recv, far_send, far_recv,
    load_sem, store_sem, send_sem, recv_sem,
):
    groups, rows, width = k_ref.shape
    heads = q_ref.shape[0]
    ratio = heads // groups
    pair = 2
    scale = 1.0 / math.sqrt(width)
    half = n_ctx // 2
    c = lax.axis_index("ctx")
    h = lax.axis_index("head")
    late = c >= half
    early = c < half
    x_dev = {"head": 1 - h}
    z_dev = {"ctx": lax.rem(c + half, n_ctx)}

    load_q = pltpu.make_async_copy(q_hbm, q_ref, load_sem.at[0])
    load_g = pltpu.make_async_copy(g_hbm, g_ref, load_sem.at[1])
    load_q.start()
    load_g.start()

    barrier = pltpu.get_barrier_semaphore()
    for dev in (x_dev, z_dev):
        pl.semaphore_signal(barrier, inc=1, device_id=dev, device_id_type=MESH)
    own_kv[:, 0] = k_ref[...]
    own_kv[:, 1] = v_ref[...]
    lse2[...] = lse_ref[...].astype(F32) * LOG2E
    delta_f[...] = delta_ref[...].astype(F32)
    pl.semaphore_wait(barrier, 2)

    def send(kind, src, dst, dev, g):
        return pltpu.make_async_remote_copy(
            src_ref=src.at[g],
            dst_ref=dst.at[g],
            send_sem=send_sem.at[kind, g],
            recv_sem=recv_sem.at[kind, g],
            device_id=dev,
            device_id_type=MESH,
        )

    def near_copy(g):
        return send(NEAR, own_kv, near_kv, x_dev, g)

    def far_copy(g):
        return send(FAR, own_kv, far_kv, z_dev, g)

    def relay_copy(g):
        return send(RELAY, far_kv, relay_kv, x_dev, g)

    def near_back(g):
        return send(NEAR_BACK, near_send, near_recv, x_dev, g)

    def swap_copy(g):
        return send(SWAP, swap_send, swap_recv, x_dev, g)

    def far_back(g):
        return send(FAR_BACK, far_send, far_recv, z_dev, g)

    ahead = 4

    @pl.when(early)
    def _():
        @pl.loop(0, groups)
        def _(g):
            far_copy(g).start()

    @pl.when(h == 0)
    def _():
        @pl.loop(0, groups)
        def _(g):
            @pl.when(early | (g < ahead))
            def _():
                near_copy(g).start()

    def unit(g, kv, diagonal, first):
        k = kv[g, 0]
        v = kv[g, 1]
        k_t = k.astype(F32).T.astype(BF16)
        dk = jnp.zeros((rows, width), F32)
        dv = jnp.zeros((rows, width), F32)
        lanes = pair * rows
        if diagonal:
            key_pos = lax.broadcasted_iota(jnp.int32, (rows, lanes), 0)
            query_pos = lax.broadcasted_iota(jnp.int32, (rows, lanes), 1) % rows
            allowed = key_pos <= query_pos
        for t in range(ratio // pair):
            head = g * ratio + t * pair
            q = q_ref[pl.ds(head, pair)].reshape(lanes, width)
            go = g_ref[pl.ds(head, pair)].reshape(lanes, width)
            lse = jnp.concatenate([lse2[pl.ds(head + i, 1), :] for i in range(pair)], 1)
            delta = jnp.concatenate([delta_f[pl.ds(head + i, 1), :] for i in range(pair)], 1)
            probs = jnp.exp2(dot(k, q, NT) * (scale * LOG2E) - lse)
            if diagonal:
                probs = jnp.where(allowed, probs, 0.0)
            dprobs = dot(v, go, NT)
            dscores = (probs * (dprobs - delta)).astype(BF16)
            dv += dot(probs.astype(BF16), go, NN)
            dk += dot(dscores, q, NN)
            dq_t = dot(k_t, dscores, NN)
            at = pl.ds(t * lanes, lanes)
            if first:
                dq_acc[g, :, at] = dq_t
            else:
                dq_acc[g, :, at] += dq_t
        return dk * scale, dv

    def finish_dq(g):
        for i in range(ratio):
            dq_t = dq_acc[g, :, pl.ds(i * rows, rows)] * scale
            dq_ref[g * ratio + i] = dq_t.T.astype(BF16)
        store_dq(g).start()

    def store_dq(g):
        at = pl.ds(g * ratio, ratio)
        return pltpu.make_async_copy(dq_ref.at[at], dq_hbm.at[at], store_sem.at[g])

    load_q.wait()
    load_g.wait()

    @pl.loop(0, groups)
    def _(g):
        dk, dv = unit(g, own_kv, True, True)
        near_acc[g, 0] = dk
        near_acc[g, 1] = dv

        @pl.when(early & (h == 0))
        def _():
            finish_dq(g)

    def near_unit(g):
        near_copy(g).wait_recv()
        dk, dv = unit(g, near_kv, False, False)
        near_send[g, 0] = dk.astype(BF16)
        near_send[g, 1] = dv.astype(BF16)
        near_back(g).start()

    @pl.when(early & (h == 1))
    def _():
        @pl.loop(0, groups)
        def _(g):
            near_unit(g)
            finish_dq(g)

    @pl.when(late)
    def _():
        @pl.loop(0, groups + 3)
        def _(t):
            @pl.when(t < groups)
            def _():
                far_copy(t).wait_recv()
                relay_copy(t).start()

                @pl.when((h == 0) & (t + ahead < groups))
                def _():
                    near_copy(t + ahead).start()

                dk, dv = unit(t, far_kv, False, False)
                far_acc[t, 0] = dk
                far_acc[t, 1] = dv

            @pl.when((t >= 1) & (t <= groups))
            def _():
                g = t - 1
                relay_copy(g).wait_recv()
                dk, dv = unit(g, relay_kv, False, False)
                swap_send[g, 0] = dk.astype(BF16)
                swap_send[g, 1] = dv.astype(BF16)
                swap_copy(g).start()
                finish_dq(g)

            @pl.when((h == 1) & (t < groups))
            def _():
                near_unit(t)

            @pl.when(t >= 3)
            def _():
                g = t - 3
                swap_copy(g).wait_recv()
                far_send[g] = (far_acc[g] + swap_recv[g].astype(F32)).astype(BF16)
                far_back(g).start()

    @pl.loop(0, groups)
    def _(g):
        @pl.when(h == 0)
        def _():
            near_back(g).wait_recv()
            near_acc[g] += near_recv[g].astype(F32)

        @pl.when(early)
        def _():
            far_back(g).wait_recv()
            near_acc[g] += far_recv[g].astype(F32)

        dk_ref[g] = near_acc[g, 0].astype(BF16)
        dv_ref[g] = near_acc[g, 1].astype(BF16)

    @pl.loop(0, groups)
    def _(g):
        store_dq(g).wait()

        @pl.when(h == 0)
        def _():
            near_copy(g).wait_send()

        @pl.when(h == 1)
        def _():
            near_back(g).wait_send()

        @pl.when(early)
        def _():
            far_copy(g).wait_send()

        @pl.when(late)
        def _():
            relay_copy(g).wait_send()
            swap_copy(g).wait_send()
            far_back(g).wait_send()


def local(queries, keys, values, delta, grad_out, lse):
    heads, rows, width = queries.shape
    groups = keys.shape[0]
    ratio = heads // groups
    n_ctx = lax.axis_size("ctx")
    block = (groups, 2, rows, width)
    vmem = pl.BlockSpec(memory_space=pltpu.VMEM)
    anywhere = pl.BlockSpec(memory_space=pl.ANY)
    return pl.pallas_call(
        functools.partial(kernel, n_ctx),
        out_shape=(
            jax.ShapeDtypeStruct(queries.shape, BF16),
            jax.ShapeDtypeStruct(keys.shape, BF16),
            jax.ShapeDtypeStruct(values.shape, BF16),
        ),
        in_specs=[anywhere, vmem, vmem, vmem, anywhere, vmem],
        out_specs=(anywhere, vmem, vmem),
        scratch_shapes=[
            pltpu.VMEM(queries.shape, BF16),
            pltpu.VMEM(queries.shape, BF16),
            pltpu.VMEM(queries.shape, BF16),
            pltpu.VMEM((groups, width, ratio * rows), F32),
            pltpu.VMEM((heads, rows), F32),
            pltpu.VMEM((heads, rows), F32),
        ]
        + [pltpu.VMEM(block, BF16)] * 4
        + [pltpu.VMEM(block, F32)] * 2
        + [pltpu.VMEM(block, BF16)] * 6
        + [
            pltpu.SemaphoreType.DMA((2,)),
            pltpu.SemaphoreType.DMA((groups,)),
            pltpu.SemaphoreType.DMA((6, groups)),
            pltpu.SemaphoreType.DMA((6, groups)),
        ],
        compiler_params=pltpu.CompilerParams(
            collective_id=0, has_side_effects=True, vmem_limit_bytes=48 * 1024 * 1024
        ),
    )(queries, keys, values, delta, grad_out, lse)


def solution(mesh):
    wide = P(None, ("ctx", "head"), None)
    flat = P(None, ("ctx", "head"))
    return jax.shard_map(
        local,
        mesh=mesh,
        in_specs=(wide, wide, wide, flat, wide, flat),
        out_specs=(wide, wide, wide),
        check_vma=False,
    )
```

time: 289 us -> 67.3 us (0.23)
  the two profiles are of different devices: /device:TPU:0 before, /device:TPU:10 now
where the time goes in v1:
time: 67.3 us; the launch traced here: 67 us
  Pallas kernels  58.7 us (87%)
  local copies, waits for them, and re-layouts  7.64 us (11%)
    pallas_call x1, Pallas kernels, local(): pl.pallas_call(functools.partial(kernel, n_ctx), out_shape=(jax.ShapeDtyp...  58.7 us
    unnamed x13, local copies, waits for them, and re-layouts  7.64 us

profile of v1, /device:TPU:10, one launch (start us, length us, event | category | flops | bytes accessed | tf_op | source)
XLA Modules:
  0.0 67.0 jit_solution(8703117106513467689)
XLA Ops:
  0.6 0.0 copy-start
  0.6 1.6 %copy-done = bf16[64,128,128]{2,1,0:T(8,128)(2,1)S(1)} copy-done((bf16[64,128,128]{2,1,0:T(8,128)(2,1)S(1)}, bf16[64,128,128]{2,1,0:T(8,128)(2,1)}, u32[]{:S(2)}) %copy-start) | copy-done | bytes 2097176
  2.2 0.0 copy-start.1
  2.2 0.9 %copy-done.1 = bf16[8,128,128]{2,1,0:T(8,128)(2,1)S(1)} copy-done((bf16[8,128,128]{2,1,0:T(8,128)(2,1)S(1)}, bf16[8,128,128]{2,1,0:T(8,128)(2,1)}, u32[]{:S(2)}) %copy-start.1) | copy-done | bytes 262168
  3.2 0.0 copy-start.2
  3.2 0.9 %copy-done.2 = bf16[8,128,128]{2,1,0:T(8,128)(2,1)S(1)} copy-done((bf16[8,128,128]{2,1,0:T(8,128)(2,1)S(1)}, bf16[8,128,128]{2,1,0:T(8,128)(2,1)}, u32[]{:S(2)}) %copy-start.2) | copy-done | bytes 262168
  4.1 0.0 copy-start.3
  4.1 0.7 %copy-done.3 = bf16[64,128]{1,0:T(8,128)(2,1)S(1)} copy-done((bf16[64,128]{1,0:T(8,128)(2,1)S(1)}, bf16[64,128]{1,0:T(8,128)(2,1)}, u32[]{:S(2)}) %copy-start.3) | copy-done | bytes 16408
  4.8 0.0 copy-start.4
  4.8 0.7 %copy-done.4 = bf16[64,128]{1,0:T(8,128)(2,1)S(1)} copy-done((bf16[64,128]{1,0:T(8,128)(2,1)S(1)}, bf16[64,128]{1,0:T(8,128)(2,1)}, u32[]{:S(2)}) %copy-start.4) | copy-done | bytes 16408
  5.6 58.7 %shard_map.85 = (bf16[64,128,128]{2,1,0:T(8,128)(2,1)S(1)}, bf16[8,128,128]{2,1,0:T(8,128)(2,1)S(1)}, bf16[8,128,128]{2,1,0:T(8,128)(2,1)S(1)}) custom-call(bf16[64,128,128]{2,1,0:T(8,128)(2,1)S(1)} %copy-done, bf16[8,128,128]{2,1,0:T(8,128)(2,1)S(1)} %copy-done.1, bf16[8,128,128]{2,1,0:T(8,128)(2,1)S(1)} %copy-done.2, bf16[64,128]{1,0:T(8,128)(2,1)S(1)} %copy-done.3, ...), custom_call_target="tpu_custom_call" | custom-call | tf_op jit(solution)/shard_map/pallas_call | solution.py:260
  64.3 1.3 %copy.12 = bf16[64,128,128]{2,1,0:T(8,128)(2,1)} copy(bf16[64,128,128]{2,1,0:T(8,128)(2,1)S(1)} %get-tuple-element.6) | data formatting | bytes 4194304
  65.6 0.7 %copy.13 = bf16[8,128,128]{2,1,0:T(8,128)(2,1)} copy(bf16[8,128,128]{2,1,0:T(8,128)(2,1)S(1)} %get-tuple-element.7) | data formatting | bytes 524288
  66.3 0.7 %copy.14 = bf16[8,128,128]{2,1,0:T(8,128)(2,1)} copy(bf16[8,128,128]{2,1,0:T(8,128)(2,1)S(1)} %get-tuple-element.8) | data formatting | bytes 524288
Async XLA Ops:
  0.6 1.6 %copy-start = (bf16[64,128,128]{2,1,0:T(8,128)(2,1)S(1)}, bf16[64,128,128]{2,1,0:T(8,128)(2,1)}, u32[]{:S(2)}) copy-start(bf16[64,128,128]{2,1,0:T(8,128)(2,1)} %q_hbm.1) | copy-start | bytes 6291460
  2.2 0.9 %copy-start.1 = (bf16[8,128,128]{2,1,0:T(8,128)(2,1)S(1)}, bf16[8,128,128]{2,1,0:T(8,128)(2,1)}, u32[]{:S(2)}) copy-start(bf16[8,128,128]{2,1,0:T(8,128)(2,1)} %k_ref.1) | copy-start | bytes 786436
  3.2 0.9 %copy-start.2 = (bf16[8,128,128]{2,1,0:T(8,128)(2,1)S(1)}, bf16[8,128,128]{2,1,0:T(8,128)(2,1)}, u32[]{:S(2)}) copy-start(bf16[8,128,128]{2,1,0:T(8,128)(2,1)} %v_ref.1) | copy-start | bytes 786436
  4.1 0.7 %copy-start.3 = (bf16[64,128]{1,0:T(8,128)(2,1)S(1)}, bf16[64,128]{1,0:T(8,128)(2,1)}, u32[]{:S(2)}) copy-start(bf16[64,128]{1,0:T(8,128)(2,1)} %delta_ref.1) | copy-start | bytes 49156
  4.8 0.7 %copy-start.4 = (bf16[64,128]{1,0:T(8,128)(2,1)S(1)}, bf16[64,128]{1,0:T(8,128)(2,1)}, u32[]{:S(2)}) copy-start(bf16[64,128]{1,0:T(8,128)(2,1)} %lse_ref.1) | copy-start | bytes 49156

commit v2 on v1

--- a/solution.py
+++ b/solution.py
@@ -25,15 +25,15 @@
 
 def kernel(
     n_ctx,
-    q_hbm, k_ref, v_ref, delta_ref, g_hbm, lse_ref,
-    dq_hbm, dk_ref, dv_ref,
-    q_ref, g_ref, dq_ref, dq_acc, lse2, delta_f,
+    q_hbm, k_hbm, v_hbm, delta_hbm, g_hbm, lse_hbm,
+    dq_hbm, dk_hbm, dv_hbm,
+    q_ref, g_ref, dq_ref, dk_ref, dv_ref, lse_ref, delta_ref, dq_acc, lse2, delta_f,
     own_kv, near_kv, far_kv, relay_kv,
     near_acc, far_acc,
     near_send, near_recv, swap_send, swap_recv, far_send, far_recv,
     load_sem, store_sem, send_sem, recv_sem,
 ):
-    groups, rows, width = k_ref.shape
+    groups, rows, width = k_hbm.shape
     heads = q_ref.shape[0]
     ratio = heads // groups
     pair = 2
@@ -46,18 +46,21 @@
     x_dev = {"head": 1 - h}
     z_dev = {"ctx": lax.rem(c + half, n_ctx)}
 
-    load_q = pltpu.make_async_copy(q_hbm, q_ref, load_sem.at[0])
-    load_g = pltpu.make_async_copy(g_hbm, g_ref, load_sem.at[1])
-    load_q.start()
-    load_g.start()
+    loads = [
+        pltpu.make_async_copy(src, dst, load_sem.at[i])
+        for i, (src, dst) in enumerate((
+            (k_hbm, own_kv.at[:, 0]), (v_hbm, own_kv.at[:, 1]), (lse_hbm, lse_ref),
+            (delta_hbm, delta_ref), (q_hbm, q_ref), (g_hbm, g_ref),
+        ))
+    ]
+    for load in loads:
+        load.start()
 
     barrier = pltpu.get_barrier_semaphore()
     for dev in (x_dev, z_dev):
         pl.semaphore_signal(barrier, inc=1, device_id=dev, device_id_type=MESH)
-    own_kv[:, 0] = k_ref[...]
-    own_kv[:, 1] = v_ref[...]
-    lse2[...] = lse_ref[...].astype(F32) * LOG2E
-    delta_f[...] = delta_ref[...].astype(F32)
+    loads[0].wait()
+    loads[1].wait()
     pl.semaphore_wait(barrier, 2)
 
     def send(kind, src, dst, dev, g):
@@ -89,6 +92,7 @@
         return send(FAR_BACK, far_send, far_recv, z_dev, g)
 
     ahead = 4
+    lead = 2
 
     @pl.when(early)
     def _():
@@ -104,17 +108,18 @@
             def _():
                 near_copy(g).start()
 
-    def unit(g, kv, diagonal, first):
-        k = kv[g, 0]
-        v = kv[g, 1]
+    def unit(g, blocks, diagonal, first):
+        k = jnp.concatenate([kv[g, 0] for kv in blocks], 0)
+        v = jnp.concatenate([kv[g, 1] for kv in blocks], 0)
         k_t = k.astype(F32).T.astype(BF16)
-        dk = jnp.zeros((rows, width), F32)
-        dv = jnp.zeros((rows, width), F32)
+        keys = len(blocks) * rows
         lanes = pair * rows
         if diagonal:
-            key_pos = lax.broadcasted_iota(jnp.int32, (rows, lanes), 0)
-            query_pos = lax.broadcasted_iota(jnp.int32, (rows, lanes), 1) % rows
+            key_pos = lax.broadcasted_iota(jnp.int32, (keys, lanes), 0) - (keys - rows)
+            query_pos = lax.broadcasted_iota(jnp.int32, (keys, lanes), 1) % rows
             allowed = key_pos <= query_pos
+        probs_half = []
+        dscores_half = []
         for t in range(ratio // pair):
             head = g * ratio + t * pair
             q = q_ref[pl.ds(head, pair)].reshape(lanes, width)
@@ -126,52 +131,66 @@
                 probs = jnp.where(allowed, probs, 0.0)
             dprobs = dot(v, go, NT)
             dscores = (probs * (dprobs - delta)).astype(BF16)
-            dv += dot(probs.astype(BF16), go, NN)
-            dk += dot(dscores, q, NN)
+            probs_half.append(probs.astype(BF16))
+            dscores_half.append(dscores)
             dq_t = dot(k_t, dscores, NN)
             at = pl.ds(t * lanes, lanes)
             if first:
                 dq_acc[g, :, at] = dq_t
             else:
                 dq_acc[g, :, at] += dq_t
-        return dk * scale, dv
+        at = pl.ds(g * ratio, ratio)
+        q = q_ref[at].reshape(ratio * rows, width)
+        go = g_ref[at].reshape(ratio * rows, width)
+        dk = dot(jnp.concatenate(dscores_half, 1), q, NN) * scale
+        dv = dot(jnp.concatenate(probs_half, 1), go, NN)
+        return dk, dv
 
     def finish_dq(g):
         for i in range(ratio):
-            dq_t = dq_acc[g, :, pl.ds(i * rows, rows)] * scale
-            dq_ref[g * ratio + i] = dq_t.T.astype(BF16)
+            dq_t = (dq_acc[g, :, pl.ds(i * rows, rows)] * scale).astype(BF16)
+            dq_ref[g * ratio + i] = dq_t.T
         store_dq(g).start()
 
     def store_dq(g):
         at = pl.ds(g * ratio, ratio)
         return pltpu.make_async_copy(dq_ref.at[at], dq_hbm.at[at], store_sem.at[g])
 
-    load_q.wait()
-    load_g.wait()
-
-    @pl.loop(0, groups)
-    def _(g):
-        dk, dv = unit(g, own_kv, True, True)
-        near_acc[g, 0] = dk
-        near_acc[g, 1] = dv
-
-        @pl.when(early & (h == 0))
-        def _():
-            finish_dq(g)
+    for load in loads[2:]:
+        load.wait()
+    lse2[...] = lse_ref[...].astype(F32) * LOG2E
+    delta_f[...] = delta_ref[...].astype(F32)
+
+    @pl.when(h == 0)
+    def _():
+        @pl.loop(0, groups)
+        def _(g):
+            dk, dv = unit(g, [own_kv], True, True)
+            near_acc[g, 0] = dk
+            near_acc[g, 1] = dv
+
+            @pl.when(early)
+            def _():
+                finish_dq(g)
 
     def near_unit(g):
         near_copy(g).wait_recv()
-        dk, dv = unit(g, near_kv, False, False)
-        near_send[g, 0] = dk.astype(BF16)
-        near_send[g, 1] = dv.astype(BF16)
+        dk, dv = unit(g, [near_kv, own_kv], True, True)
+        near_acc[g, 0] = dk[rows:]
+        near_acc[g, 1] = dv[rows:]
+        near_send[g, 0] = dk[:rows].astype(BF16)
+        near_send[g, 1] = dv[:rows].astype(BF16)
         near_back(g).start()
 
-    @pl.when(early & (h == 1))
-    def _():
-        @pl.loop(0, groups)
+    @pl.when(h == 1)
+    def _():
+        @pl.loop(0, jnp.where(early, groups, lead))
         def _(g):
             near_unit(g)
-            finish_dq(g)
+
+            @pl.when(early)
+            def _():
+                finish_dq(g)
 
     @pl.when(late)
     def _():
@@ -186,23 +205,21 @@
                 def _():
                     near_copy(t + ahead).start()
 
-                dk, dv = unit(t, far_kv, False, False)
-                far_acc[t, 0] = dk
-                far_acc[t, 1] = dv
-
             @pl.when((t >= 1) & (t <= groups))
             def _():
                 g = t - 1
                 relay_copy(g).wait_recv()
-                dk, dv = unit(g, relay_kv, False, False)
-                swap_send[g, 0] = dk.astype(BF16)
-                swap_send[g, 1] = dv.astype(BF16)
+                dk, dv = unit(g, [far_kv, relay_kv], False, False)
+                swap_send[g, 0] = dk[rows:].astype(BF16)
+                swap_send[g, 1] = dv[rows:].astype(BF16)
                 swap_copy(g).start()
+                far_acc[g, 0] = dk[:rows]
+                far_acc[g, 1] = dv[:rows]
                 finish_dq(g)
 
-            @pl.when((h == 1) & (t < groups))
-            def _():
-                near_unit(t)
+            @pl.when((h == 1) & (t + lead < groups))
+            def _():
+                near_unit(t + lead)
 
             @pl.when(t >= 3)
             def _():
@@ -226,6 +243,13 @@
         dk_ref[g] = near_acc[g, 0].astype(BF16)
         dv_ref[g] = near_acc[g, 1].astype(BF16)
 
+    stores = [
+        pltpu.make_async_copy(dk_ref, dk_hbm, load_sem.at[0]),
+        pltpu.make_async_copy(dv_ref, dv_hbm, load_sem.at[1]),
+    ]
+    for store in stores:
+        store.start()
+
     @pl.loop(0, groups)
     def _(g):
         store_dq(g).wait()
@@ -247,6 +271,21 @@
             relay_copy(g).wait_send()
             swap_copy(g).wait_send()
             far_back(g).wait_send()
+
+    for store in stores:
+        store.wait()
+
+
+def write_out(*refs):
+    sem = refs[-1]
+    count = len(refs) // 2
+    copies = [
+        pltpu.make_async_copy(refs[i], refs[count + i], sem.at[i]) for i in range(count)
+    ]
+    for copy in copies:
+        copy.start()
+    for copy in copies:
+        copy.wait()
 
 
 def local(queries, keys, values, delta, grad_out, lse):
@@ -255,21 +294,24 @@
     ratio = heads // groups
     n_ctx = lax.axis_size("ctx")
     block = (groups, 2, rows, width)
-    vmem = pl.BlockSpec(memory_space=pltpu.VMEM)
     anywhere = pl.BlockSpec(memory_space=pl.ANY)
-    return pl.pallas_call(
+    grads = pl.pallas_call(
         functools.partial(kernel, n_ctx),
         out_shape=(
             jax.ShapeDtypeStruct(queries.shape, BF16),
             jax.ShapeDtypeStruct(keys.shape, BF16),
             jax.ShapeDtypeStruct(values.shape, BF16),
         ),
-        in_specs=[anywhere, vmem, vmem, vmem, anywhere, vmem],
-        out_specs=(anywhere, vmem, vmem),
+        in_specs=[anywhere] * 6,
+        out_specs=(anywhere,) * 3,
         scratch_shapes=[
             pltpu.VMEM(queries.shape, BF16),
             pltpu.VMEM(queries.shape, BF16),
             pltpu.VMEM(queries.shape, BF16),
+            pltpu.VMEM(keys.shape, BF16),
+            pltpu.VMEM(keys.shape, BF16),
+            pltpu.VMEM(lse.shape, BF16),
+            pltpu.VMEM(lse.shape, BF16),
             pltpu.VMEM((groups, width, ratio * rows), F32),
             pltpu.VMEM((heads, rows), F32),
             pltpu.VMEM((heads, rows), F32),
@@ -278,15 +320,23 @@
         + [pltpu.VMEM(block, F32)] * 2
         + [pltpu.VMEM(block, BF16)] * 6
         + [
-            pltpu.SemaphoreType.DMA((2,)),
+            pltpu.SemaphoreType.DMA((6,)),
             pltpu.SemaphoreType.DMA((groups,)),
             pltpu.SemaphoreType.DMA((6, groups)),
             pltpu.SemaphoreType.DMA((6, groups)),
         ],
         compiler_params=pltpu.CompilerParams(
-            collective_id=0, has_side_effects=True, vmem_limit_bytes=48 * 1024 * 1024
+            collective_id=0, has_side_effects=True, vmem_limit_bytes=60 * 1024 * 1024
         ),
     )(queries, keys, values, delta, grad_out, lse)
+    return pl.pallas_call(
+        write_out,
+        out_shape=tuple(jax.ShapeDtypeStruct(x.shape, x.dtype) for x in grads),
+        in_specs=[anywhere] * 3,
+        out_specs=(anywhere,) * 3,
+        scratch_shapes=[pltpu.SemaphoreType.DMA((3,))],
+        compiler_params=pltpu.CompilerParams(vmem_limit_bytes=60 * 1024 * 1024),
+    )(*grads)
 
 
 def solution(mesh):

time: 67.3 us -> 140 us (2.08)
  Pallas kernels: 58.7 us -> 139 us
  local copies, waits for them, and re-layouts: 7.64 us -> 0 us
    pallas_call x0 -> x1, Pallas kernels: none -> 80.5 us  [local(): pl.pallas_call(write_out, out_shape=tuple((jax.ShapeDtypeStruct(x.shape,...]
    unnamed x13 -> x0, local copies, waits for them, and re-layouts: 7.64 us -> none
where the time goes in v2:
time: 140 us
  Pallas kernels  139 us (99%)
    pallas_call x1, Pallas kernels, local(): pl.pallas_call(write_out, out_shape=tuple((jax.ShapeDtypeStruct(x.shape,...  80.5 us
    pallas_call x1, Pallas kernels, local(): pl.pallas_call(functools.partial(kernel, n_ctx), out_shape=(jax.ShapeDtyp...  58.6 us

profile of v2, /device:TPU:10, one launch (start us, length us, event | category | flops | bytes accessed | tf_op | source)
XLA Modules:
  0.0 139.7 jit_solution(15447387028540315208)
XLA Ops:
  0.6 58.6 %shard_map.85 = (bf16[64,128,128]{2,1,0:T(8,128)(2,1)}, bf16[8,128,128]{2,1,0:T(8,128)(2,1)}, bf16[8,128,128]{2,1,0:T(8,128)(2,1)}) custom-call(bf16[64,128,128]{2,1,0:T(8,128)(2,1)} %q_hbm.1, bf16[8,128,128]{2,1,0:T(8,128)(2,1)} %k_hbm.1, bf16[8,128,128]{2,1,0:T(8,128)(2,1)} %v_hbm.1, bf16[64,128]{1,0:T(8,128)(2,1)} %delta_hbm.1, ...), custom_call_target="tpu_custom_call" | custom-call | tf_op jit(solution)/shard_map/pallas_call | solution.py:298
  59.2 80.5 %shard_map.86 = (bf16[64,128,128]{2,1,0:T(8,128)(2,1)}, bf16[8,128,128]{2,1,0:T(8,128)(2,1)}, bf16[8,128,128]{2,1,0:T(8,128)(2,1)}) custom-call(bf16[64,128,128]{2,1,0:T(8,128)(2,1)} %get-tuple-element.6.refs_0_, bf16[8,128,128]{2,1,0:T(8,128)(2,1)} %get-tuple-element.7.refs_1_, bf16[8,128,128]{2,1,0:T(8,128)(2,1)} %get-tuple-element.8.refs_2_), custom_call_target="tpu_custom_call" | custom-call | tf_op jit(solution)/shard_map/pallas_call | solution.py:332

commit v3 on v2

--- a/solution.py
+++ b/solution.py
@@ -12,7 +12,8 @@
 BF16 = jnp.bfloat16
 MESH = pl.DeviceIdType.MESH
 LOG2E = 1.0 / math.log(2.0)
-NEAR, FAR, RELAY, NEAR_BACK, SWAP, FAR_BACK = range(6)
+KINDS = 7
+NEAR, FAR, RELAY, NEAR_BACK, SWAP, FAR_BACK, OTHER = range(KINDS)
 
 
 def dot(a, b, dims):
@@ -94,19 +95,47 @@
     ahead = 4
     lead = 2
 
+    def around_copy(g):
+        return send(RELAY, near_kv, relay_kv, z_dev, g)
+
+    def other_back(g):
+        return send(OTHER, swap_send, relay_kv, z_dev, g)
+
+    def other_swap(g):
+        return send(SWAP, relay_kv, swap_recv, x_dev, g)
+
+    def by_early(g):
+        return lax.rem(g, 3) == 2
+
+    def back_apart(g):
+        return lax.rem(g, 4) == 0
+
     @pl.when(early)
     def _():
         @pl.loop(0, groups)
         def _(g):
+            @pl.when(by_early(g))
+            def _():
+                near_copy(g).start()
+
+        @pl.loop(0, groups)
+        def _(g):
             far_copy(g).start()
 
-    @pl.when(h == 0)
-    def _():
-        @pl.loop(0, groups)
-        def _(g):
-            @pl.when(early | (g < ahead))
+            @pl.when((h == 0) & jnp.logical_not(by_early(g)))
             def _():
                 near_copy(g).start()
+
+            @pl.when(by_early(g))
+            def _():
+                near_copy(g).wait_recv()
+                around_copy(g).start()
+
+    @pl.when(late & (h == 0))
+    def _():
+        @pl.loop(0, ahead)
+        def _(g):
+            near_copy(g).start()
 
     def unit(g, blocks, diagonal, first):
         k = jnp.concatenate([kv[g, 0] for kv in blocks], 0)
@@ -174,7 +203,10 @@
                 finish_dq(g)
 
     def near_unit(g):
-        near_copy(g).wait_recv()
+        @pl.when(late | jnp.logical_not(by_early(g)))
+        def _():
+            near_copy(g).wait_recv()
+
         dk, dv = unit(g, [near_kv, own_kv], True, True)
         near_acc[g, 0] = dk[rows:]
         near_acc[g, 1] = dv[rows:]
@@ -199,7 +231,10 @@
             @pl.when(t < groups)
             def _():
                 far_copy(t).wait_recv()
-                relay_copy(t).start()
+
+                @pl.when(jnp.logical_not(by_early(t)))
+                def _():
+                    relay_copy(t).start()
 
                 @pl.when((h == 0) & (t + ahead < groups))
                 def _():
@@ -212,22 +247,42 @@
                 dk, dv = unit(g, [far_kv, relay_kv], False, False)
                 swap_send[g, 0] = dk[rows:].astype(BF16)
                 swap_send[g, 1] = dv[rows:].astype(BF16)
-                swap_copy(g).start()
-                far_acc[g, 0] = dk[:rows]
-                far_acc[g, 1] = dv[:rows]
+
+                @pl.when(back_apart(g))
+                def _():
+                    other_back(g).start()
+                    far_send[g, 0] = dk[:rows].astype(BF16)
+                    far_send[g, 1] = dv[:rows].astype(BF16)
+                    far_back(g).start()
+
+                @pl.when(jnp.logical_not(back_apart(g)))
+                def _():
+                    swap_copy(g).start()
+                    far_acc[g, 0] = dk[:rows]
+                    far_acc[g, 1] = dv[:rows]
+
                 finish_dq(g)
 
             @pl.when((h == 1) & (t + lead < groups))
             def _():
                 near_unit(t + lead)
 
-            @pl.when(t >= 3)
+            @pl.when((t >= 3) & jnp.logical_not(back_apart(t - 3)))
             def _():
                 g = t - 3
                 swap_copy(g).wait_recv()
                 far_send[g] = (far_acc[g] + swap_recv[g].astype(F32)).astype(BF16)
                 far_back(g).start()
 
+    @pl.when(early)
+    def _():
+        @pl.loop(0, groups)
+        def _(g):
+            @pl.when(back_apart(g))
+            def _():
+                other_back(g).wait_recv()
+                other_swap(g).start()
+
     @pl.loop(0, groups)
     def _(g):
         @pl.when(h == 0)
@@ -239,6 +294,11 @@
         def _():
             far_back(g).wait_recv()
             near_acc[g] += far_recv[g].astype(F32)
+
+            @pl.when(back_apart(g))
+            def _():
+                other_swap(g).wait_recv()
+                near_acc[g] += swap_recv[g].astype(F32)
 
         dk_ref[g] = near_acc[g, 0].astype(BF16)
         dv_ref[g] = near_acc[g, 1].astype(BF16)
@@ -254,7 +314,7 @@
     def _(g):
         store_dq(g).wait()
 
-        @pl.when(h == 0)
+        @pl.when((h == 0) | (early & by_early(g)))
         def _():
             near_copy(g).wait_send()
 
@@ -266,26 +326,57 @@
         def _():
             far_copy(g).wait_send()
 
+        @pl.when(early & by_early(g))
+        def _():
+            around_copy(g).wait_send()
+
+        @pl.when(early & back_apart(g))
+        def _():
+            other_swap(g).wait_send()
+
         @pl.when(late)
         def _():
+            far_back(g).wait_send()
+
+        @pl.when(late & jnp.logical_not(by_early(g)))
+        def _():
             relay_copy(g).wait_send()
+
+        @pl.when(late & back_apart(g))
+        def _():
+            other_back(g).wait_send()
+
+        @pl.when(late & jnp.logical_not(back_apart(g)))
+        def _():
             swap_copy(g).wait_send()
-            far_back(g).wait_send()
 
     for store in stores:
         store.wait()
 
 
-def write_out(*refs):
-    sem = refs[-1]
-    count = len(refs) // 2
-    copies = [
-        pltpu.make_async_copy(refs[i], refs[count + i], sem.at[i]) for i in range(count)
-    ]
-    for copy in copies:
-        copy.start()
-    for copy in copies:
-        copy.wait()
+def write_out(parts, *refs):
+    count = len(parts)
+    sources, results, staged = refs[:count], refs[count:2 * count], refs[2 * count:3 * count]
+    read_sem, write_sem = refs[3 * count:]
+    reads, writes = [], []
+    for i, cuts in enumerate(parts):
+        size = sources[i].shape[0] // cuts
+        for j in range(cuts):
+            at = pl.ds(j * size, size)
+            n = len(reads)
+            reads.append(
+                pltpu.make_async_copy(sources[i].at[at], staged[i].at[at], read_sem.at[n])
+            )
+            writes.append(
+                pltpu.make_async_copy(staged[i].at[at], results[i].at[at], write_sem.at[n])
+            )
+    for read in reads:
+        read.start()
+    for read, write in zip(reads, writes):
+        read.wait()
+        write.start()
+    for write in writes:
+        write.wait()
 
 
 def local(queries, keys, values, delta, grad_out, lse):
@@ -322,19 +413,21 @@
         + [
             pltpu.SemaphoreType.DMA((6,)),
             pltpu.SemaphoreType.DMA((groups,)),
-            pltpu.SemaphoreType.DMA((6, groups)),
-            pltpu.SemaphoreType.DMA((6, groups)),
+            pltpu.SemaphoreType.DMA((KINDS, groups)),
+            pltpu.SemaphoreType.DMA((KINDS, groups)),
         ],
         compiler_params=pltpu.CompilerParams(
             collective_id=0, has_side_effects=True, vmem_limit_bytes=60 * 1024 * 1024
         ),
     )(queries, keys, values, delta, grad_out, lse)
+    parts = (4, 1, 1)
     return pl.pallas_call(
-        write_out,
+        functools.partial(write_out, parts),
         out_shape=tuple(jax.ShapeDtypeStruct(x.shape, x.dtype) for x in grads),
         in_specs=[anywhere] * 3,
         out_specs=(anywhere,) * 3,
-        scratch_shapes=[pltpu.SemaphoreType.DMA((3,))],
+        scratch_shapes=[pltpu.VMEM(x.shape, x.dtype) for x in grads]
+        + [pltpu.SemaphoreType.DMA((sum(parts),))] * 2,
         compiler_params=pltpu.CompilerParams(vmem_limit_bytes=60 * 1024 * 1024),
     )(*grads)
 

time: 140 us -> 60.8 us (0.43)
  Pallas kernels: 139 us -> 60 us
    pallas_call x1, Pallas kernels: 80.5 us -> 2.63 us  [local(): pl.pallas_call(functools.partial(write_out, parts), out_shape=tuple((jax....]
where the time goes in v3:
time: 60.8 us; the launch traced here: 60.6 us
  Pallas kernels  60 us (99%)
  between operations  0.64 us (1%)
    pallas_call x1, Pallas kernels, local(): pl.pallas_call(functools.partial(kernel, n_ctx), out_shape=(jax.ShapeDtyp...  57.4 us
    pallas_call x1, Pallas kernels, local(): pl.pallas_call(functools.partial(write_out, parts), out_shape=tuple((jax....  2.63 us

profile of v3, /device:TPU:10, one launch (start us, length us, event | category | flops | bytes accessed | tf_op | source)
XLA Modules:
  0.0 60.6 jit_solution(16374792746769330473)
XLA Ops:
  0.6 57.4 %shard_map.85 = (bf16[64,128,128]{2,1,0:T(8,128)(2,1)}, bf16[8,128,128]{2,1,0:T(8,128)(2,1)}, bf16[8,128,128]{2,1,0:T(8,128)(2,1)}) custom-call(bf16[64,128,128]{2,1,0:T(8,128)(2,1)} %q_hbm.1, bf16[8,128,128]{2,1,0:T(8,128)(2,1)} %k_hbm.1, bf16[8,128,128]{2,1,0:T(8,128)(2,1)} %v_hbm.1, bf16[64,128]{1,0:T(8,128)(2,1)} %delta_hbm.1, ...), custom_call_target="tpu_custom_call" | custom-call | tf_op jit(solution)/shard_map/pallas_call | solution.py:389
  58.0 2.6 %shard_map.86 = (bf16[64,128,128]{2,1,0:T(8,128)(2,1)}, bf16[8,128,128]{2,1,0:T(8,128)(2,1)}, bf16[8,128,128]{2,1,0:T(8,128)(2,1)}) custom-call(bf16[64,128,128]{2,1,0:T(8,128)(2,1)} %get-tuple-element.6.refs_0_, bf16[8,128,128]{2,1,0:T(8,128)(2,1)} %get-tuple-element.7.refs_1_, bf16[8,128,128]{2,1,0:T(8,128)(2,1)} %get-tuple-element.8.refs_2_), custom_call_target="tpu_custom_call" | custom-call | tf_op jit(solution)/shard_map/pallas_call | solution.py:424

commit v4 on v3

--- a/solution.py
+++ b/solution.py
@@ -92,8 +92,9 @@
     def far_back(g):
         return send(FAR_BACK, far_send, far_recv, z_dev, g)
 
-    ahead = 4
+    ahead = 3
     lead = 2
+    flying = 2
 
     def around_copy(g):
         return send(RELAY, near_kv, relay_kv, z_dev, g)
@@ -110,26 +111,25 @@
     def back_apart(g):
         return lax.rem(g, 4) == 0
 
+    def issue(g):
+        far_copy(g).start()
+
+        @pl.when(by_early(g))
+        def _():
+            near_copy(g).wait_recv()
+            around_copy(g).start()
+
     @pl.when(early)
     def _():
         @pl.loop(0, groups)
         def _(g):
-            @pl.when(by_early(g))
+            @pl.when(by_early(g) | ((h == 0) & (g == 0)))
             def _():
                 near_copy(g).start()
 
-        @pl.loop(0, groups)
-        def _(g):
-            far_copy(g).start()
-
-            @pl.when((h == 0) & jnp.logical_not(by_early(g)))
-            def _():
-                near_copy(g).start()
-
-            @pl.when(by_early(g))
-            def _():
-                near_copy(g).wait_recv()
-                around_copy(g).start()
+        @pl.loop(0, flying)
+        def _(g):
+            issue(g)
 
     @pl.when(late & (h == 0))
     def _():
@@ -190,18 +190,6 @@
     lse2[...] = lse_ref[...].astype(F32) * LOG2E
     delta_f[...] = delta_ref[...].astype(F32)
 
-    @pl.when(h == 0)
-    def _():
-        @pl.loop(0, groups)
-        def _(g):
-            dk, dv = unit(g, [own_kv], True, True)
-            near_acc[g, 0] = dk
-            near_acc[g, 1] = dv
-
-            @pl.when(early)
-            def _():
-                finish_dq(g)
-
     def near_unit(g):
         @pl.when(late | jnp.logical_not(by_early(g)))
         def _():
@@ -214,15 +202,43 @@
         near_send[g, 1] = dv[:rows].astype(BF16)
         near_back(g).start()
 
-    @pl.when(h == 1)
-    def _():
-        @pl.loop(0, jnp.where(early, groups, lead))
-        def _(g):
+    def near_step(g):
+        @pl.when(h == 0)
+        def _():
+            dk, dv = unit(g, [own_kv], True, True)
+            near_acc[g, 0] = dk
+            near_acc[g, 1] = dv
+
+        @pl.when(h == 1)
+        def _():
             near_unit(g)
 
-            @pl.when(early)
-            def _():
-                finish_dq(g)
+    @pl.when(early)
+    def _():
+        @pl.loop(0, groups)
+        def _(g):
+            far_copy(g).wait_send()
+
+            @pl.when(by_early(g))
+            def _():
+                around_copy(g).wait_send()
+
+            @pl.when(g + flying < groups)
+            def _():
+                issue(g + flying)
+
+            @pl.when((h == 0) & (g + 1 < groups) & jnp.logical_not(by_early(g + 1)))
+            def _():
+                near_copy(g + 1).start()
+
+            near_step(g)
+            finish_dq(g)
+
+    @pl.when(late)
+    def _():
+        @pl.loop(0, lead)
+        def _(g):
+            near_step(g)
 
     @pl.when(late)
     def _():
@@ -263,9 +279,9 @@
 
                 finish_dq(g)
 
-            @pl.when((h == 1) & (t + lead < groups))
-            def _():
-                near_unit(t + lead)
+            @pl.when(t + lead < groups)
+            def _():
+                near_step(t + lead)
 
             @pl.when((t >= 3) & jnp.logical_not(back_apart(t - 3)))
             def _():
@@ -321,14 +337,6 @@
         @pl.when(h == 1)
         def _():
             near_back(g).wait_send()
-
-        @pl.when(early)
-        def _():
-            far_copy(g).wait_send()
-
-        @pl.when(early & by_early(g))
-        def _():
-            around_copy(g).wait_send()
 
         @pl.when(early & back_apart(g))
         def _():

time: 60.8 us -> 60.8 us (level)
  no operation moved by 1% of the time
where the time goes in v4:
time: 60.8 us; the launch traced here: 60.1 us
  Pallas kernels  59.4 us (98%)
  between operations  0.64 us (1%)
    pallas_call x1, Pallas kernels, local(): pl.pallas_call(functools.partial(kernel, n_ctx), out_shape=(jax.ShapeDtyp...  56.8 us
    pallas_call x1, Pallas kernels, local(): pl.pallas_call(functools.partial(write_out, parts), out_shape=tuple((jax....  2.63 us

profile of v4, /device:TPU:10, one launch (start us, length us, event | category | flops | bytes accessed | tf_op | source)
XLA Modules:
  0.0 60.1 jit_solution(2169547495790319894)
XLA Ops:
  0.6 56.8 %shard_map.85 = (bf16[64,128,128]{2,1,0:T(8,128)(2,1)}, bf16[8,128,128]{2,1,0:T(8,128)(2,1)}, bf16[8,128,128]{2,1,0:T(8,128)(2,1)}) custom-call(bf16[64,128,128]{2,1,0:T(8,128)(2,1)} %q_hbm.1, bf16[8,128,128]{2,1,0:T(8,128)(2,1)} %k_hbm.1, bf16[8,128,128]{2,1,0:T(8,128)(2,1)} %v_hbm.1, bf16[64,128]{1,0:T(8,128)(2,1)} %delta_hbm.1, ...), custom_call_target="tpu_custom_call" | custom-call | tf_op jit(solution)/shard_map/pallas_call | solution.py:397
  57.4 2.6 %shard_map.86 = (bf16[64,128,128]{2,1,0:T(8,128)(2,1)}, bf16[8,128,128]{2,1,0:T(8,128)(2,1)}, bf16[8,128,128]{2,1,0:T(8,128)(2,1)}) custom-call(bf16[64,128,128]{2,1,0:T(8,128)(2,1)} %get-tuple-element.6.refs_0_, bf16[8,128,128]{2,1,0:T(8,128)(2,1)} %get-tuple-element.7.refs_1_, bf16[8,128,128]{2,1,0:T(8,128)(2,1)} %get-tuple-element.8.refs_2_), custom_call_target="tpu_custom_call" | custom-call | tf_op jit(solution)/shard_map/pallas_call | solution.py:432

commit v5 on v4

--- a/solution.py
+++ b/solution.py
@@ -106,10 +106,10 @@
         return send(SWAP, relay_kv, swap_recv, x_dev, g)
 
     def by_early(g):
-        return lax.rem(g, 3) == 2
+        return lax.rem(g, 8) == 5
 
     def back_apart(g):
-        return lax.rem(g, 4) == 0
+        return lax.rem(g, 8) == 4
 
     def issue(g):
         far_copy(g).start()

time: 60.8 us -> 61.4 us (level)
  Pallas kernels: 59.4 us -> 60.6 us
    pallas_call x1, Pallas kernels: 56.8 us -> 58 us  [local(): pl.pallas_call(functools.partial(kernel, n_ctx), out_shape=(jax.ShapeDtyp...]
where the time goes in v5:
time: 61.4 us; the launch traced here: 61.3 us
  Pallas kernels  60.6 us (99%)
  between operations  0.64 us (1%)
    pallas_call x1, Pallas kernels, local(): pl.pallas_call(functools.partial(kernel, n_ctx), out_shape=(jax.ShapeDtyp...  58 us
    pallas_call x1, Pallas kernels, local(): pl.pallas_call(functools.partial(write_out, parts), out_shape=tuple((jax....  2.63 us

profile of v5, /device:TPU:10, one launch (start us, length us, event | category | flops | bytes accessed | tf_op | source)
XLA Modules:
  0.0 61.3 jit_solution(15686031057195967610)
XLA Ops:
  0.6 58.0 %shard_map.85 = (bf16[64,128,128]{2,1,0:T(8,128)(2,1)}, bf16[8,128,128]{2,1,0:T(8,128)(2,1)}, bf16[8,128,128]{2,1,0:T(8,128)(2,1)}) custom-call(bf16[64,128,128]{2,1,0:T(8,128)(2,1)} %q_hbm.1, bf16[8,128,128]{2,1,0:T(8,128)(2,1)} %k_hbm.1, bf16[8,128,128]{2,1,0:T(8,128)(2,1)} %v_hbm.1, bf16[64,128]{1,0:T(8,128)(2,1)} %delta_hbm.1, ...), custom_call_target="tpu_custom_call" | custom-call | tf_op jit(solution)/shard_map/pallas_call | solution.py:397
  58.6 2.6 %shard_map.86 = (bf16[64,128,128]{2,1,0:T(8,128)(2,1)}, bf16[8,128,128]{2,1,0:T(8,128)(2,1)}, bf16[8,128,128]{2,1,0:T(8,128)(2,1)}) custom-call(bf16[64,128,128]{2,1,0:T(8,128)(2,1)} %get-tuple-element.6.refs_0_, bf16[8,128,128]{2,1,0:T(8,128)(2,1)} %get-tuple-element.7.refs_1_, bf16[8,128,128]{2,1,0:T(8,128)(2,1)} %get-tuple-element.8.refs_2_), custom_call_target="tpu_custom_call" | custom-call | tf_op jit(solution)/shard_map/pallas_call | solution.py:432

commit v6 on v4

--- a/solution.py
+++ b/solution.py
@@ -94,7 +94,7 @@
 
     ahead = 3
     lead = 2
-    flying = 2
+    flying = jnp.where(c * 4 >= n_ctx, 4, 2)
 
     def around_copy(g):
         return send(RELAY, near_kv, relay_kv, z_dev, g)

time: 60.8 us -> 60.8 us (level)
  no operation moved by 1% of the time
where the time goes in v6:
time: 60.8 us; the launch traced here: 60.1 us
  Pallas kernels  59.4 us (98%)
  between operations  0.64 us (1%)
    pallas_call x1, Pallas kernels, local(): pl.pallas_call(functools.partial(kernel, n_ctx), out_shape=(jax.ShapeDtyp...  56.8 us
    pallas_call x1, Pallas kernels, local(): pl.pallas_call(functools.partial(write_out, parts), out_shape=tuple((jax....  2.63 us

profile of v6, /device:TPU:10, one launch (start us, length us, event | category | flops | bytes accessed | tf_op | source)
XLA Modules:
  0.0 60.1 jit_solution(9185394139886871550)
XLA Ops:
  0.6 56.8 %shard_map.85 = (bf16[64,128,128]{2,1,0:T(8,128)(2,1)}, bf16[8,128,128]{2,1,0:T(8,128)(2,1)}, bf16[8,128,128]{2,1,0:T(8,128)(2,1)}) custom-call(bf16[64,128,128]{2,1,0:T(8,128)(2,1)} %q_hbm.1, bf16[8,128,128]{2,1,0:T(8,128)(2,1)} %k_hbm.1, bf16[8,128,128]{2,1,0:T(8,128)(2,1)} %v_hbm.1, bf16[64,128]{1,0:T(8,128)(2,1)} %delta_hbm.1, ...), custom_call_target="tpu_custom_call" | custom-call | tf_op jit(solution)/shard_map/pallas_call | solution.py:397
  57.4 2.6 %shard_map.86 = (bf16[64,128,128]{2,1,0:T(8,128)(2,1)}, bf16[8,128,128]{2,1,0:T(8,128)(2,1)}, bf16[8,128,128]{2,1,0:T(8,128)(2,1)}) custom-call(bf16[64,128,128]{2,1,0:T(8,128)(2,1)} %get-tuple-element.6.refs_0_, bf16[8,128,128]{2,1,0:T(8,128)(2,1)} %get-tuple-element.7.refs_1_, bf16[8,128,128]{2,1,0:T(8,128)(2,1)} %get-tuple-element.8.refs_2_), custom_call_target="tpu_custom_call" | custom-call | tf_op jit(solution)/shard_map/pallas_call | solution.py:432
